TPU v7x, 32 devices: a whole 2x2x4 slice. The times are simulated.
32 devices in a mesh: groups: 2 (over y), slab: 16 (over z, x, core).
Axes of the slice: x: 2, y: 2, z: 4, core: 2. Of those that a mesh axis runs over, the one named last changes fastest.
Arguments:
- volume: bfloat16 [4096, 32, 2048], P(('groups', 'slab')), parts along dimension 0, may hold values from 0 to 2
- measured: bfloat16 [32, 512, 2048], P(('groups', 'slab')), parts along dimension 0, may hold values from 0 to 80
- path_weights: bfloat16 [16, 32], replicated, may hold values from 0.25 to 1
- fractions: float32 [16, 2048], replicated, may hold values from 0.1 to 0.5
- bases: int32 [16], replicated, may hold values from 1 to 1536, as said below
Outputs:
- new_volume: float32 [4096, 32, 2048], P(('groups', 'slab')), parts along dimension 0
There are 2 independent parts, one for each index of `groups`. A program takes and returns all parts, laid end to end along the dimension named above; an argument that names none is the same for every part. Nothing has to cross between parts.
Inputs may be any that keep to these rules, and one draw needn't show every extreme that they name: `bases`: the entries, taken in increasing order, begin with 1 and end with 1536, and consecutive ones differ by less than 512; every slice lies within, or directly before, the rows of some projection. The order of the projections along the subset is not that of the helix.
All inputs are finite; a program needn't handle non-finite values.
Results may differ from a plain program's by a relative error of at most 0.002.
Values may be sent and summed in bfloat16 or wider, within the bound.
No kernel may reach another device: no remote copies, remote signals or barrier semaphores. Data moves between devices by JAX's collectives and lax.ppermute only.
A program may use at most 192 MiB of HBM per device.

v0:
```python
import functools

import jax
import jax.numpy as jnp
from jax import lax
from jax.experimental import pallas as pl
from jax.experimental.pallas import tpu as pltpu
from jax.sharding import PartitionSpec as P

RELAX = 1.0
BLOCK = 16
HALF = 8
LANES = 128
WIDE = 256
PIECES = 4
PARTS = 2
ROUTED_CLASSES = 4
LOAD = 2
CODE = 256
LINES = 5
VMEM_LIMIT = 56 * 2**20


def dot(a, b):
    return jnp.dot(a, b, preferred_element_type=jnp.float32)


def widen(coef):
    return jnp.concatenate([coef] * (WIDE // LANES), axis=1)


def spread_out(own, arrived):
    views = list(enumerate(own))
    return views + [(s * LOAD + n, p.at[n]) for s, p in enumerate(arrived) for n in range(p.shape[0])]


def update_kernel(
    dense, part, table_ref, lower_ref, upper_ref, next_ref, right_ref, coef_ref, image_w_ref, weight_ref, spread_ref, *rest
):
    if dense:
        left_ref, edge_ref, edge_coef_ref, *rest = rest
    out_ref, carry_ref, seen_ref, result_ref, sems, out_sems = rest[-6:]
    packets = rest[:-7]
    block = pl.program_id(0)
    blocks = pl.num_programs(0)
    depth, width = lower_ref.shape[1:]
    angles = weight_ref.shape[0]
    first = part * blocks * BLOCK

    def fetch(at_block, act):
        slot = at_block % 2
        rows = pl.ds(pl.multiple_of(at_block * BLOCK, BLOCK), BLOCK)
        if dense:
            act(pltpu.make_async_copy(packets[0].at[:, rows], seen_ref.at[slot], sems.at[slot, 0]))
            return
        middle = (len(packets) - ROUTED_CLASSES) // 2 + ROUTED_CLASSES
        views = [(4, *v) for v in spread_out(packets[:ROUTED_CLASSES], [])]
        views += [(2, *v) for v in spread_out([], packets[ROUTED_CLASSES:middle])]
        views += [(3, *v) for v in spread_out([], packets[middle:])]
        for n, (line, spot, view) in enumerate(views):
            name = table_ref[part * LINES + line, spot]

            @pl.when(name >= 0)
            def _():
                act(pltpu.make_async_copy(view.at[rows], seen_ref.at[slot, name], sems.at[slot, n]))

    def deliver(at_block, act, pieces=range(PIECES)):
        slot = at_block % 2
        rows = pl.ds(first + at_block * BLOCK, BLOCK)
        for n in pieces:
            at = pl.ds(n * (width // PIECES), width // PIECES)
            act(pltpu.make_async_copy(result_ref.at[slot, :, :, at], out_ref.at[rows, :, at], out_sems.at[slot, n]))

    @pl.when(block == 0)
    def _():
        seen_ref[...] = jnp.zeros_like(seen_ref)
        fetch(block, lambda copy: copy.start())

    @pl.when(block + 1 < blocks)
    def _():
        fetch(block + 1, lambda copy: copy.start())

    @pl.when(block == 0)
    def _():
        if not dense:
            carry_ref[...] = jnp.zeros_like(carry_ref)
            return
        for chunk in range(width // WIDE):
            at = pl.ds(chunk * WIDE, WIDE)
            mine = dot(weight_ref[...], lower_ref[0, :, at])
            before = dot(weight_ref[...], left_ref[0, :, at])
            carry_ref[:, at] = (
                edge_ref[:, at].astype(jnp.float32) * widen(edge_coef_ref[2])
                - mine * widen(edge_coef_ref[0])
                - before * widen(edge_coef_ref[1])
            ).astype(jnp.bfloat16)

    @pl.when(block >= 2)
    def _():
        deliver(block - 2, lambda copy: copy.wait())

    fetch(block, lambda copy: copy.wait())
    slot = block % 2
    final = (block == blocks - 1) & (part == PARTS - 1 or dense)

    def columns(chunk):
        if dense:
            return pl.ds(pl.multiple_of(chunk * WIDE, WIDE), WIDE)
        return slice(chunk * WIDE, (chunk + 1) * WIDE)

    def image(chunk):
        at = columns(chunk)
        images = [dot(image_w_ref[...], r[:, :, at].reshape(HALF * depth, WIDE)) for r in (lower_ref, upper_ref)]
        after = dot(weight_ref[...], jnp.where(final, right_ref[0, :, at], next_ref[0, :, at]))
        return images, after

    def residual(chunk, images, after):
        at = columns(chunk)
        seen = seen_ref[slot, :, :, at].astype(jnp.float32)
        ahead = [pltpu.roll(x.reshape(angles, HALF, WIDE), HALF - 1, 1) for x in images]
        ahead.append(jnp.broadcast_to(after.reshape(angles, 1, WIDE), (angles, HALF, WIDE)))
        tail = lax.broadcasted_iota(jnp.int32, (angles, HALF, WIDE), 1) == HALF - 1
        parts = []
        for half in range(2):
            now = jnp.where(tail, ahead[half + 1], ahead[half]).reshape(angles * HALF, WIDE)
            got = seen[:, half * HALF : (half + 1) * HALF].reshape(angles * HALF, WIDE)
            coef = [widen(coef_ref[0, half, n]) for n in range(3)]
            resid = got * coef[2] - now * coef[0] - images[half] * coef[1]
            parts.append(resid.reshape(angles, HALF, WIDE))
        return parts

    def result(chunk, parts):
        at = columns(chunk)
        carry = carry_ref[:, at]
        for half, (resid, r) in enumerate(zip(parts, (lower_ref, upper_ref))):
            inputs = jnp.concatenate([resid.reshape(angles * HALF, WIDE).astype(jnp.bfloat16), carry])
            spread = dot(spread_ref[half], inputs).reshape(HALF, depth, WIDE)
            carry = resid[:, HALF - 1].astype(jnp.bfloat16)
            result_ref[slot, half * HALF : (half + 1) * HALF, :, at] = r[:, :, at].astype(jnp.float32) + spread
        carry_ref[:, at] = carry

    chunks = width // WIDE
    if dense:
        pl.loop(0, chunks)(lambda chunk: result(chunk, residual(chunk, *image(chunk))))
        deliver(block, lambda copy: copy.start())
    else:
        images, resids = {}, {}
        for n in range(chunks + 2):
            if n < chunks:
                images[n] = image(n)
            if 1 <= n <= chunks:
                resids[n - 1] = residual(n - 1, *images.pop(n - 1))
            if n >= 2:
                result(n - 2, resids.pop(n - 2))
                done = (n - 1) * PIECES
                if done % chunks == 0:
                    deliver(block, lambda copy: copy.start(), [done // chunks - 1])

    @pl.when(block == blocks - 1)
    def _():
        @pl.when(block >= 1)
        def _():
            deliver(block - 1, lambda copy: copy.wait())

        deliver(block, lambda copy: copy.wait())


def update(volume, right, tables, packets, table, before, part, parts, ahead=None):
    slices, depth, cols = volume.shape
    dense = ahead is not None
    blocks = slices // BLOCK // parts
    off = part * blocks
    by_block = lambda x: pl.BlockSpec((1,) + x.shape[1:], lambda b, i: (b,) + (0,) * (x.ndim - 1))
    whole = lambda x: pl.BlockSpec(x.shape, lambda b, i: (0,) * x.ndim)
    anywhere = pl.BlockSpec(memory_space=pl.ANY)
    coef, edge_coef, image_w, weights, spread_w = tables
    angles = weights.shape[0]
    ahead = [*ahead, edge_coef] if dense else []
    held = jax.ShapeDtypeStruct((angles, cols), volume.dtype)
    if before is None:
        before = coef
    aliases = {9 + len(ahead) + len(packets): 0} if before.shape == volume.shape else {}
    copies = LOAD * len(packets)
    one = (1, depth, cols)
    return pl.pallas_call(
        functools.partial(update_kernel, dense, part),
        grid_spec=pltpu.PrefetchScalarGridSpec(
            num_scalar_prefetch=1,
            grid=(blocks,),
            in_specs=[
                pl.BlockSpec((HALF, depth, cols), lambda b, i: (2 * (b + off), 0, 0)),
                pl.BlockSpec((HALF, depth, cols), lambda b, i: (2 * (b + off) + 1, 0, 0)),
                pl.BlockSpec(one, lambda b, i: (jnp.minimum((b + off + 1) * BLOCK, slices - 1), 0, 0)),
                whole(right), by_block(coef), whole(image_w), whole(weights),
                pl.BlockSpec((2,) + spread_w.shape[1:], lambda b, i: (b, 0, 0)),
            ]
            + [whole(x) for x in ahead]
            + [anywhere] * (len(packets) + 1),
            out_specs=[anywhere, whole(held)],
            scratch_shapes=[
                pltpu.VMEM((2, angles, BLOCK, cols), jnp.bfloat16),
                pltpu.VMEM((2, BLOCK, depth, cols), jnp.float32),
                pltpu.SemaphoreType.DMA((2, copies)),
                pltpu.SemaphoreType.DMA((2, PIECES)),
            ],
        ),
        out_shape=[jax.ShapeDtypeStruct(volume.shape, jnp.float32), held],
        input_output_aliases=aliases,
        compiler_params=pltpu.CompilerParams(dimension_semantics=("arbitrary",), vmem_limit_bytes=VMEM_LIMIT),
        cost_estimate=pl.CostEstimate(
            flops=4 * slices * depth * cols * angles // parts, bytes_accessed=volume.size * 7 // parts, transcendentals=0
        ),
        name="slab_update",
    )(
        table, volume, volume, volume, right, coef, image_w, weights, spread_w, *ahead, *packets, before
    )


def mend_kernel(lower_ref, upper_ref, first_ref, second_ref, before_ref, out_ref):
    columns = lower_ref.shape[2] - first_ref.shape[0]

    @pl.when(pl.program_id(0) == 0)
    def _():
        out_ref[0] = before_ref[0] + dot(lower_ref[0, :, columns:], first_ref[...])

    @pl.when(pl.program_id(0) == 1)
    def _():
        out_ref[0] = before_ref[0] + dot(upper_ref[0, :, columns:], second_ref[...])


def mend(out, lower, upper, first, second):
    slices, depth, cols = out.shape
    whole = pl.BlockSpec(first.shape, lambda b: (0, 0))
    weights = pl.BlockSpec((1, depth, lower.shape[2]), lambda b: (0, 0, 0))
    slab = pl.BlockSpec((1, depth, cols), lambda b: (b * (slices // 2), 0, 0))
    return pl.pallas_call(
        mend_kernel,
        grid=(2,),
        in_specs=[weights, weights, whole, whole, slab],
        out_specs=slab,
        out_shape=jax.ShapeDtypeStruct(out.shape, out.dtype),
        input_output_aliases={4: 0},
        name="mend_slices",
    )(lower, upper, first, second, out)


def fill_weights(wide_w, turned_w, pick_next, pick_now, pick_carry, spread_ref, half):
    depth, columns = wide_w.shape
    place = lax.broadcasted_iota(jnp.int32, (depth, columns), 1) % HALF
    from_next = wide_w * pick_next
    from_now = wide_w * pick_now
    from_carry = turned_w * pick_carry
    for z in range(HALF):
        row = jnp.where(place == z, from_next, jnp.where(place == z - 1, from_now, 0.0))
        total = jnp.sum(row, axis=1, keepdims=True)
        carry = jnp.zeros_like(from_carry)
        if z == 0:
            total = total + jnp.sum(from_carry, axis=1, keepdims=True)
            carry = from_carry
        scale = RELAX / total
        spread_ref[half, z * depth : (z + 1) * depth, :columns] = (row * scale).astype(jnp.bfloat16)
        spread_ref[half, z * depth : (z + 1) * depth, columns:] = (carry * scale).astype(jnp.bfloat16)


def weights_kernel(wide_w_ref, turned_w_ref, pick_ref, pick_carry_ref, spread_ref):
    picks = pick_ref[0, 0:1], pick_ref[0, 1:2], pick_carry_ref[0]
    fill_weights(wide_w_ref[...], turned_w_ref[...], *picks, spread_ref, 0)


def make_weights(wide_w, turned_w, pick, pick_carry):
    halves = pick.shape[0]
    depth, angles = turned_w.shape
    by_half = lambda shape: pl.BlockSpec((1,) + shape, lambda b: (b,) + (0,) * len(shape))
    whole = lambda x: pl.BlockSpec(x.shape, lambda b: (0,) * x.ndim)
    spread = (HALF * depth, angles * (HALF + 1))
    return pl.pallas_call(
        weights_kernel,
        grid=(halves,),
        in_specs=[whole(wide_w), whole(turned_w), by_half(pick.shape[1:]), by_half(pick_carry.shape[1:])],
        out_specs=by_half(spread),
        out_shape=jax.ShapeDtypeStruct((halves,) + spread, jnp.bfloat16),
        name="spread_weights",
    )(wide_w, turned_w, pick, pick_carry)


def make_tables(share, first, rows, path_weights, bases, slices):
    angles, depth = path_weights.shape
    blocks = slices // BLOCK
    weights = path_weights.astype(jnp.float32)
    ray_total = jnp.sum(weights, axis=1)[:, None]
    norm = 1.0 / (ray_total * ((1.0 - share[:, 1:]) + share[:, :-1]))
    coefs = jnp.stack([(1.0 - share[:, 1:]) * norm, share[:, :-1] * norm, norm])
    coef = coefs[:, :, 1:].reshape(3, angles, blocks, BLOCK // HALF, HALF).transpose(2, 3, 0, 1, 4)
    coef = coef.reshape(blocks, BLOCK // HALF, 3, angles * HALF, 1)
    coef = jnp.broadcast_to(coef, coef.shape[:4] + (LANES,))
    edge_coef = jnp.broadcast_to(coefs[:, :, :1], (3, angles, LANES))
    share_own = share[:, 1:-1]
    row_now = (first - bases)[:, None] + jnp.arange(slices, dtype=jnp.int32)[None, :]
    w_now = jnp.where((row_now >= 0) & (row_now < rows), 1.0 - share_own, 0.0)
    w_next = jnp.where((row_now + 1 >= 0) & (row_now + 1 < rows), share_own, 0.0)
    halves = slices // HALF
    pick = jnp.stack([w_next, jnp.pad(w_now[:, 1:], ((0, 0), (0, 1)))]).reshape(2, angles, halves, HALF)
    pick = pick.transpose(2, 0, 1, 3).reshape(halves, 2, angles * HALF)
    pick_carry = w_now[:, ::HALF].T[:, None, :]
    eye = jnp.eye(HALF, dtype=jnp.float32)
    image_w = jnp.einsum("ad,yz->ayzd", weights, eye).reshape(angles * HALF, HALF * depth).astype(jnp.bfloat16)
    wide_w = jnp.repeat(weights.T, HALF, axis=1)
    return coef, edge_coef, image_w, path_weights, make_weights(wide_w, weights.T, pick, pick_carry)


def column_of(line, tall):
    sub = lax.broadcasted_iota(jnp.int32, (tall, LANES), 0)
    lane = lax.broadcasted_iota(jnp.int32, (tall, LANES), 1)
    return jnp.max(jnp.where(sub == lane, line, -1), axis=1, keepdims=True)


def tables_kernel(rows, off, base_piece, device_ref, bases_ref, own_ref, after_ref, weight_ref, *rest):
    if base_piece:
        coef_ref, spread_ref, image_w_ref, wide_ref, turned_ref = rest
    else:
        coef_ref, spread_ref, wide_ref, turned_ref = rest[2:]
    block = pl.program_id(0) + off
    angles, depth = weight_ref.shape
    first = device_ref[0] * LANES
    shape = (angles, LANES)
    lane = lax.broadcasted_iota(jnp.int32, shape, 1)
    sub = lax.broadcasted_iota(jnp.int32, shape, 0)
    weights = weight_ref[...].astype(jnp.float32)
    ray_total = jnp.sum(weights, axis=1, keepdims=True)
    own = own_ref[...]
    ahead = jnp.where(lane == LANES - 1, pltpu.roll(after_ref[...], LANES - 1, 1), pltpu.roll(own, LANES - 1, 1))
    norm = 1.0 / (ray_total * ((1.0 - ahead) + own))
    coefs = ((1.0 - ahead) * norm, own * norm, norm)
    spots = lax.broadcasted_iota(jnp.int32, (angles, HALF, LANES), 2) - lax.broadcasted_iota(jnp.int32, (angles, HALF, LANES), 1)
    for half in range(BLOCK // HALF):
        here = spots == block * BLOCK + half * HALF
        for n, coef in enumerate(coefs):
            tall = jnp.broadcast_to(coef.reshape(angles, 1, LANES), (angles, HALF, LANES))
            tall = jnp.sum(jnp.where(here, tall, 0.0), axis=2, keepdims=True)
            coef_ref[0, half, n] = jnp.broadcast_to(tall, (angles, HALF, LANES)).reshape(angles * HALF, LANES)

    def fill_image_weights():
        across = (HALF * depth)
        repeat = lax.broadcasted_iota(jnp.int32, (depth, across), 1) % depth
        repeat = jnp.where(repeat == lax.broadcasted_iota(jnp.int32, (depth, across), 0), 1.0, 0.0)
        wide = dot(weight_ref[...], repeat.astype(jnp.bfloat16)).astype(jnp.bfloat16)
        down = angles * HALF
        expand = lax.broadcasted_iota(jnp.int32, (down, angles), 0) // HALF
        expand = jnp.where(expand == lax.broadcasted_iota(jnp.int32, (down, angles), 1), 1.0, 0.0)
        wide = dot(expand.astype(jnp.bfloat16), wide)
        at = lax.broadcasted_iota(jnp.int32, (down, across), 0) % HALF
        same = lax.broadcasted_iota(jnp.int32, (down, across), 1) // depth == at
        image_w_ref[...] = jnp.where(same, wide, 0.0).astype(jnp.bfloat16)

    if base_piece:
        pl.when(block == off)(fill_image_weights)
    row_now = first + lane - column_of(bases_ref[...], angles)
    w_now = jnp.where((row_now >= 0) & (row_now < rows), 1.0 - own, 0.0)
    w_next = jnp.where((row_now + 1 >= 0) & (row_now + 1 < rows), own, 0.0)
    columns = angles * HALF
    mine = lax.broadcasted_iota(jnp.int32, (angles, columns), 1) // HALF
    mine = mine == lax.broadcasted_iota(jnp.int32, (angles, columns), 0)
    square = lax.broadcasted_iota(jnp.int32, (angles, angles), 0) == lax.broadcasted_iota(jnp.int32, (angles, angles), 1)

    def gather(values, start, count):
        near = jnp.where(lane < count, pltpu.roll(values, (2 * LANES - start) % LANES, 1), 0.0)
        step = HALF
        while step < LANES:
            near = near + pltpu.roll(near, step, 1)
            step *= 2
        return jnp.sum(jnp.where(mine, near, 0.0), axis=0, keepdims=True)

    turned = lambda other: lax.dot_general(
        weights, other, (((0,), (0,)), ((), ())), precision=lax.Precision.HIGHEST, preferred_element_type=jnp.float32
    )

    @pl.when(block == off)
    def _():
        wide_ref[...] = turned(jnp.where(mine, 1.0, 0.0))
        turned_ref[...] = turned(jnp.where(square, 1.0, 0.0))

    for half in range(BLOCK // HALF):
        start = block * BLOCK + half * HALF
        pick_next = gather(w_next, start, HALF)
        pick_now = gather(w_now, start + 1, HALF - 1)
        carry = jnp.sum(jnp.where(lane == start, w_now, 0.0), axis=1, keepdims=True)
        pick_carry = jnp.sum(jnp.where(square, carry, 0.0), axis=0, keepdims=True)
        fill_weights(wide_ref[...], turned_ref[...], pick_next, pick_now, pick_carry, spread_ref, half)


def device_tables(device, row_of_bases, fractions, path_weights, rows, part, piece, made=None):
    angles, depth = path_weights.shape
    blocks = LANES // BLOCK // PARTS
    steps = blocks // 2
    here = piece * steps
    last = fractions.shape[1] // LANES - 1
    column = lambda by: pl.BlockSpec((angles, LANES), lambda b, d: (0, jnp.clip(d[0] + by, 0, last)))
    whole = lambda shape: pl.BlockSpec(shape, lambda b, d: (0,) * len(shape))
    coef = (BLOCK // HALF, 3, angles * HALF, LANES)
    image_w = (angles * HALF, HALF * depth)
    spread = (HALF * depth, angles * (HALF + 1))
    out_specs = [
        pl.BlockSpec((1,) + coef, lambda b, d: (b + here, 0, 0, 0, 0)),
        pl.BlockSpec((2,) + spread, lambda b, d: (b + here, 0, 0)),
    ]
    out_shape = [
        jax.ShapeDtypeStruct((blocks,) + coef, jnp.float32),
        jax.ShapeDtypeStruct((2 * blocks,) + spread, jnp.bfloat16),
    ]
    if made is None:
        out_specs.append(whole(image_w))
        out_shape.append(jax.ShapeDtypeStruct(image_w, jnp.bfloat16))
    filled = [] if made is None else [made[0], made[4]]
    done = pl.pallas_call(
        functools.partial(tables_kernel, rows, part * blocks + here, made is None),
        grid_spec=pltpu.PrefetchScalarGridSpec(
            num_scalar_prefetch=1,
            grid=(steps,),
            in_specs=[whole((1, LANES)), column(0), column(1), whole(path_weights.shape)]
            + [pl.BlockSpec(memory_space=pl.ANY)] * len(filled),
            out_specs=out_specs,
            scratch_shapes=[
                pltpu.VMEM((depth, angles * HALF), jnp.float32),
                pltpu.VMEM((depth, angles), jnp.float32),
            ],
        ),
        out_shape=out_shape,
        input_output_aliases={5 + n: n for n in range(len(filled))},
        name="make_tables",
    )(device, row_of_bases, fractions, fractions, path_weights, *filled)
    return done[0], None, done[2] if made is None else made[2], path_weights, done[1]


def turn_kernel(classes, count, part, device_ref, bases_ref, seen_ref, volume_ref, *refs):
    *outs, slice_ref, twice_ref, sems = refs
    pltpu.make_async_copy(volume_ref.at[pl.ds(0, 1)], slice_ref, sems.at[2]).start()
    rows, cols = seen_ref.shape
    more = twice_ref.shape[0] - rows
    copies = [
        pltpu.make_async_copy(seen_ref, twice_ref.at[pl.ds(0, rows)], sems.at[0]),
        pltpu.make_async_copy(seen_ref.at[pl.ds(0, more)], twice_ref.at[pl.ds(rows, more)], sems.at[1]),
    ]
    for copy in copies:
        copy.start()
    for copy in copies:
        copy.wait()
    device = device_ref[0]
    base = bases_ref[device]
    my_class = device & (classes - 1)
    slices = count * PARTS

    def window(place, size, at):
        start = (place - base + 1 + rows) & (rows - 1)
        begin = pl.multiple_of(start & ~(BLOCK - 1), BLOCK)
        tall = size + BLOCK
        wide = twice_ref[pl.ds(begin, tall), at].astype(jnp.float32)
        return pltpu.roll(wide, (tall - (start - begin)) % tall, 0)

    for n, out in enumerate(outs):
        place = (my_class ^ n) * slices + part * count

        @pl.loop(0, cols // WIDE)
        def _(chunk):
            at = pl.ds(pl.multiple_of(chunk * WIDE, WIDE), WIDE)
            out[:, at] = window(place, count, at)[:count].astype(jnp.bfloat16)

    pltpu.make_async_copy(volume_ref.at[pl.ds(0, 1)], slice_ref, sems.at[2]).wait()


def turn(device, bases, seen, volume, classes, part):
    rows, cols = seen.shape
    count = rows // classes // PARTS
    return pl.pallas_call(
        functools.partial(turn_kernel, classes, count, part),
        in_specs=[
            pl.BlockSpec(memory_space=pltpu.SMEM),
            pl.BlockSpec(memory_space=pltpu.SMEM),
            pl.BlockSpec(memory_space=pl.ANY),
            pl.BlockSpec(memory_space=pl.ANY),
        ],
        out_specs=[pl.BlockSpec(memory_space=pltpu.VMEM)] * (classes + 1),
        out_shape=[jax.ShapeDtypeStruct((count, cols), seen.dtype)] * classes
        + [jax.ShapeDtypeStruct((1,) + volume.shape[1:], volume.dtype)],
        scratch_shapes=[pltpu.VMEM((rows + count + BLOCK, cols), seen.dtype), pltpu.SemaphoreType.DMA((3,))],
        compiler_params=pltpu.CompilerParams(vmem_limit_bytes=32 * 2**20),
        name="turn_rows",
    )(device, bases, seen, volume)


def plan_kernel(slots, planes, classes, angles, count, rows, ends, device_ref, bases_ref, table_ref, which_ref):
    shape = (2 * PARTS * classes, LANES)
    lane = lax.broadcasted_iota(jnp.int32, shape, 1)
    row = lax.broadcasted_iota(jnp.int32, shape, 0)
    class_shift = classes.bit_length() - 1
    base = jnp.broadcast_to(bases_ref[...], shape) - 1
    low_plane = base >> (rows.bit_length() - 1)
    turned = base & (rows - 1)

    def reach(which):
        lowest = low_plane + jnp.where(which * count + count - 1 < turned, 1, 0)
        highest = low_plane + jnp.where(which * count < turned, 1, 0)
        return lowest, highest

    lowest, highest = reach(row >> 1)
    upward = (row & 1) == 0
    source = lane >> class_shift
    at = jnp.where(upward, source, planes - 1 - source)
    to = jnp.where(lane < angles, jnp.where(upward, highest, planes - 1 - lowest), -1)
    key = to * CODE + (CODE - 1 - lane)
    sent = [jnp.full(shape, -1, jnp.int32) for _ in range(planes - 1)]
    for slot in range(slots):
        begin = at
        for link in range(planes - 1):
            ready = (begin == link) & (to > link)
            for n in range(LOAD):
                best = jnp.max(jnp.where(ready, key, -1), axis=1, keepdims=True)
                taken = ready & (key == best)
                at = jnp.where(taken, link + 1, at)
                ready = ready & (key != best)
                which = jnp.where(best >= 0, CODE - 1 - (best & (CODE - 1)), -1)
                sent[link] = jnp.where(lane == slot * LOAD + n, which, sent[link])

    me = device_ref[0]
    my_class = me & (classes - 1)
    plane = me >> class_shift
    none = jnp.full(shape, -1, jnp.int32)
    used = none
    for link in range(planes - 1):
        used = jnp.maximum(used, sent[link])
    used = jnp.max(used, axis=0, keepdims=True)
    head = lane[:1]
    need = jnp.max(jnp.where(used >= 0, head + 1, 0))
    need = jnp.where(jnp.max(to - at) > 0, slots * LOAD + 1, need)
    which_ref[0] = sum(jnp.where(need > end, 1, 0) for end in ends)

    tall = -(-max(slots * LOAD, angles) // 8) * 8
    sub = lax.broadcasted_iota(jnp.int32, (tall, LANES), 0)
    held = jnp.where(head < classes, plane * classes + (head ^ my_class), -1)
    for part in range(PARTS):
        low_here, high_here = reach(my_class * PARTS + part)
        wanted = (plane >= low_here) & (plane <= high_here) & (lane < angles)
        wanted = column_of(jnp.where(wanted, 1, 0)[:1], tall) > 0
        keep = lambda ids: jnp.max(jnp.where((sub == ids) & wanted, ids, -1), axis=0, keepdims=True)
        moves = []
        for way, spot in ((0, plane), (1, planes - 1 - plane)):
            sends, gets = none, none
            for link in range(planes - 1):
                sends = jnp.where(spot == link, sent[link], sends)
                gets = jnp.where(spot == link + 1, sent[link], gets)
            mine = row == 2 * (my_class * PARTS + part) + way
            sends = jnp.max(jnp.where(mine, sends, -1), axis=0, keepdims=True)
            gets = jnp.max(jnp.where(mine, gets, -1), axis=0, keepdims=True)
            arrived = jnp.max(jnp.where((column_of(gets, tall) == sends) & (sends >= 0), sub, 0), axis=0, keepdims=True)
            own = (sends >> class_shift) == plane
            index = jnp.where(own, (sends & (classes - 1)) ^ my_class, classes + arrived)
            moves.append((jnp.where(sends >= 0, index, 0), keep(gets)))
        for exchange in range(2):
            upward = ((plane + exchange) & 1) == 0
            line = part * LINES + exchange
            table_ref[line : line + 1] = jnp.where(upward, moves[0][0], moves[1][0])
            table_ref[line + 2 : line + 3] = jnp.where(upward, moves[1][1], moves[0][1])
        line = part * LINES + 4
        table_ref[line : line + 1] = keep(held)


def choose_kernel(slot, part, load, own, ups, table_ref, *refs):
    sources, (*outs, sems) = refs[: own + 2 * ups], refs[own + 2 * ups :]
    arrived = sources[own + ups :], sources[own : own + ups]
    views = [spread_out(sources[:own], []) + [(own + n, v) for n, v in spread_out([], side)] for side in arrived]
    spots = [(way, n) for way in range(2) for n in range(load)]
    for way, n in spots:
        for m, view in views[way]:

            @pl.when(table_ref[part * LINES + way, slot * LOAD + n] == m)
            def _():
                pltpu.make_async_copy(view, outs[way].at[n], sems.at[way, n]).start()

    for way, n in spots:
        pltpu.make_async_copy(sources[0], outs[way].at[n], sems.at[way, n]).wait()


def choose(slot, part, load, table, own, ups, downs):
    anywhere = pl.BlockSpec(memory_space=pl.ANY)
    shape = jax.ShapeDtypeStruct((load,) + own[0].shape, own[0].dtype)
    return pl.pallas_call(
        functools.partial(choose_kernel, slot, part, load, len(own), len(ups)),
        in_specs=[pl.BlockSpec(memory_space=pltpu.SMEM)] + [anywhere] * (len(own) + 2 * len(ups)),
        out_specs=[pl.BlockSpec(memory_space=pltpu.VMEM)] * 2,
        out_shape=[shape, shape],
        scratch_shapes=[pltpu.SemaphoreType.DMA((2, load))],
        cost_estimate=pl.CostEstimate(flops=0, bytes_accessed=4 * load * own[0].size * 2, transcendentals=0),
        name="choose_packet",
    )(table, *own, *ups, *downs)


def on_device(volume, measured, path_weights, fractions, bases):
    slices, depth, cols = volume.shape
    local, rows = measured.shape[:2]
    nslab = lax.axis_size("slab")
    device = lax.axis_index("slab")
    angles = local * nslab
    first = device * slices
    classes = rows // slices
    planes = nslab // classes
    pairs = [(i, i + classes) for i in range(nslab - classes)]
    pairs = [[p for p in pairs if p[0] // classes % 2 == odd] for odd in range(2)]
    pairs = [p + [(j, i) for i, j in p] for p in pairs]
    ups_of = lambda step: [(i, i + step) for i in range(nslab - step)]
    downs_of = lambda step: [(i + step, i) for i in range(nslab - step)]

    routed = local == 1 and classes == ROUTED_CLASSES and slices == LANES and rows & (rows - 1) == 0 and angles * HALF == LANES

    def dense(volume, measured, path_weights, fractions, bases):
        left = lax.ppermute(volume[slices - 1 :], "slab", ups_of(1))
        right = lax.ppermute(volume[:1], "slab", downs_of(1))
        share = lax.dynamic_slice_in_dim(jnp.pad(fractions, ((0, 0), (1, 1))), first, slices + 2, 1)
        tables = make_tables(share, first, rows, path_weights, bases, slices)
        my_bases = lax.dynamic_slice_in_dim(bases, device * local, local, 0)
        turned = jax.vmap(lambda m, b: jnp.roll(m, b - 1, axis=0))(measured, my_bases)
        by_class = turned.reshape(local, classes, slices, cols).transpose(1, 0, 2, 3)
        outgoing = jnp.tile(by_class, (planes, 1, 1, 1)).reshape(angles, slices, cols)
        seen = lax.all_to_all(outgoing, "slab", split_axis=0, concat_axis=0, tiled=True)
        ends = jnp.roll(by_class[:, :, slices - 1], 1, axis=0)
        ends = jnp.tile(ends, (planes, 1, 1)).reshape(angles, cols // LANES, LANES)
        edge = lax.all_to_all(ends, "slab", split_axis=0, concat_axis=0, tiled=True).reshape(angles, cols)
        return update(volume, right, tables, [seen], jnp.zeros((8, LANES), jnp.int32), None, 0, 1, (left, edge))[0]

    if not routed:
        return dense(volume, measured, path_weights, fractions, bases)

    number = device.astype(jnp.int32)[None]
    upper, lower = PARTS - 1, 0
    exchange = lambda runs: [runs[0]] + [
        lax.ppermute(runs[d], "slab", [(i, i ^ d) for i in range(nslab)]) for d in range(1, classes)
    ]
    *runs, high = turn(number, bases, measured[0], volume, classes, upper)
    runs, late_bases, seen = lax.optimization_barrier((runs, bases, measured[0]))
    own = {upper: exchange(runs)}

    row_of_bases = jnp.pad(late_bases, (0, LANES - angles), constant_values=1)[None]
    ends = [5, 6, 7]
    most = -(-ends[-1] // LOAD)
    table, which = pl.pallas_call(
        functools.partial(plan_kernel, most, planes, classes, angles, slices // PARTS, rows, ends),
        in_specs=[pl.BlockSpec(memory_space=pltpu.SMEM), pl.BlockSpec(memory_space=pltpu.VMEM)],
        out_specs=[pl.BlockSpec(memory_space=pltpu.VMEM), pl.BlockSpec(memory_space=pltpu.SMEM)],
        out_shape=[jax.ShapeDtypeStruct((16, LANES), jnp.int32), jax.ShapeDtypeStruct((1,), jnp.int32)],
        name="plan_slots",
    )(number, row_of_bases)
    table, which, high = lax.optimization_barrier((table, which, high))
    right = lax.ppermute(high, "slab", downs_of(1))
    *runs, _ = turn(number, bases, seen, volume, classes, lower)
    tables = device_tables(number, row_of_bases, fractions, path_weights, rows, upper, 0)
    tables = [tables[0], *tables[2:]]
    arrived, runs, table, tables, right = lax.optimization_barrier((own[upper], runs, table, tables, right))

    def finish(end):
        def branch(arrived, runs, table, upper_tables, right):
            own = {upper: arrived, lower: exchange(runs)}
            first, other = {upper: [], lower: []}, {upper: [], lower: []}
            late = row_of_bases
            tables = {upper: (upper_tables[0], None, *upper_tables[1:]), lower: None}
            beside = {(0, upper): (upper, 1), (1, upper): (lower, 0), (1, lower): (lower, 1)}
            for slot in range(-(-end // LOAD)):
                load = min(LOAD, end - slot * LOAD)
                for part in (upper, lower):
                    go_first, go_other = choose(slot, part, load, table, own[part], first[part], other[part])
                    if (slot, part) in beside:
                        go_first, go_other, late = lax.optimization_barrier((go_first, go_other, late))
                        where, piece = beside[slot, part]
                        made = device_tables(number, late, fractions, path_weights, rows, where, piece, tables[where])
                        table, made = lax.optimization_barrier((table, made))
                        tables[where] = made
                    first[part].append(lax.ppermute(go_first, "slab", pairs[0]))
                    other[part].append(lax.ppermute(go_other, "slab", pairs[1]))
            packets = {part: own[part] + first[part] + other[part] for part in (upper, lower)}
            out, last = update(volume, right, tables[upper], packets[upper], table, None, upper, PARTS)
            ahead = lax.ppermute(last, "slab", ups_of(1))
            out, second = update(volume, right, tables[lower], packets[lower], table, out, lower, PARTS)
            return mend(out, tables[lower][-1], tables[upper][-1], ahead, second)

        return branch

    others = lambda *_: dense(volume, measured, path_weights, fractions, bases)
    return lax.switch(which[0], [finish(e) for e in ends] + [others], arrived, runs, table, tables, right)


def solution(mesh):
    placed = (P(("groups", "slab"), None, None), P(("groups", "slab"), None, None), P(), P(), P())
    return jax.shard_map(
        on_device,
        mesh=mesh,
        in_specs=placed,
        out_specs=P(("groups", "slab"), None, None),
        check_vma=False,
    )
```

profile of v0, /device:TPU:15, one launch (start us, length us, event | category | flops | bytes accessed | tf_op | source)
XLA Modules:
  0.0 273.2 jit_solution(9196717088968470526)
XLA Ops:
  0.0 4.4 %turn_rows.2 = (bf16[64,2048]{1,0:T(8,128)(2,1)}, bf16[64,2048]{1,0:T(8,128)(2,1)S(1)}, bf16[64,2048]{1,0:T(8,128)(2,1)S(1)}, bf16[64,2048]{1,0:T(8,128)(2,1)S(1)}, bf16[1,32,2048]{2,1,0:T(8,128)(2,1)S(1)}) custom-call(s32[1]{0:T(128)} %bitcast.24.device_ref, s32[16]{0:T(128)} %bases_ref.3, bf16[512,2048]{1,0:T(8,128)(2,1)} %bitcast.54, ...), custom_call_target="tpu_custom_call" | custom-call | tf_op jit(solution)/shard_map/turn_rows/pallas_call | solution.py:473
  4.4 0.7 collective-permute-start.54
  5.2 0.3 collective-permute-start.55
  5.4 1.4 collective-permute-start.56
  6.9 2.0 plan_slots.1
  8.9 2.1 collective-permute-start.57
  11.0 3.2 %make_tables.19 = (f32[4,2,3,128,128]{4,3,2,1,0:T(8,128)S(1)}, bf16[8,256,144]{2,1,0:T(8,128)(2,1)S(1)}, bf16[128,256]{1,0:T(8,128)(2,1)}) custom-call(s32[1]{0:T(128)} %bitcast.24.device_ref, s32[1,128]{1,0:T(1,128)S(1)} %pad_bitcast_fusion.1.bases_ref, f32[16,2048]{1,0:T(8,128)} %after_ref.1, f32[16,2048]{1,0:T(8,128)} %after_ref.1, ...), custom_call_target="tpu_custom_call" | custom-call | tf_op jit(solution)/shard_map/make_tables/pallas_call | solution.py:414
  14.2 4.6 %turn_rows.3 = (bf16[64,2048]{1,0:T(8,128)(2,1)}, bf16[64,2048]{1,0:T(8,128)(2,1)}, bf16[64,2048]{1,0:T(8,128)(2,1)}, bf16[64,2048]{1,0:T(8,128)(2,1)}, bf16[1,32,2048]{2,1,0:T(8,128)(2,1)}) custom-call(s32[1]{0:T(128)} %bitcast.24.device_ref, s32[16]{0:T(128)} %bases_ref.3, bf16[512,2048]{1,0:T(8,128)(2,1)} %bitcast.55, bf16[128,32,2048]{2,1,0:T(8,128)(2,1)} %volume_ref.3), custom_call_target="tpu_custom_call" | custom-call | tf_op jit(solution)/shard_map/turn_rows/pallas_call | solution.py:473
  19.3 1.0 collective-permute-done.56
  20.3 252.7 %conditional.1 = (f32[128,32,2048]{2,1,0:T(8,128)}) conditional(s32[]{:T(128)} %bitcast.27, (s32[16,128]{1,0:T(8,128)S(1)}, bf16[64,2048]{1,0:T(8,128)(2,1)}, bf16[64,2048]{1,0:T(8,128)(2,1)}, bf16[64,2048]{1,0:T(8,128)(2,1)}, bf16[64,2048]{1,0:T(8,128)(2,1)}, /*index=5*/s32[1,128]{1,0:T(1,128)S(1)}, s32[1]{0:T(128)}, ...), branch_computations={%region_0.1_spmd, %region_1.2_spmd, %region_2.3_spmd, %region_3.5_... | conditional | flops 541218752 | bytes 112460800 | solution.py:685
  20.3 1.2 dynamic_slice.5
  22.2 3.5 %fusion = bf16[1,512,2048]{2,1,0:T(8,128)(2,1)S(1)} fusion(s32[]{:T(128)} %bitcast.15, bf16[1,512,2048]{2,1,0:T(8,128)(2,1)} %get-tuple-element.333), kind=kLoop, calls=%fused_computation.2 | loop fusion | flops 4194304 | bytes 4194308 | tf_op jit(solution)/shard_map/cond/branch_3_fun/vmap(jit(_roll_dynamic))/concatenate | solution.py:619
  26.0 10.0 %all_to_all.8 = bf16[16,16,128]{2,1,0:T(8,128)(2,1)S(1)} all-to-all(bf16[16,16,128]{2,1,0:T(8,128)(2,1)S(1)} %tile.5), channel_id=1, replica_groups=mesh['groups'=2,'slab'=16] {'slab'}, dimensions={0} | all-to-all | bytes 131072 | tf_op jit(solution)/shard_map/cond/branch_3_fun/all_to_all | solution.py:625
  35.9 4.5 %tile.19 = bf16[4,4,128,2048]{3,2,1,0:T(8,128)(2,1)} broadcast(bf16[4,128,2048]{2,1,0:T(8,128)(2,1)S(1)} %bitcast.58), dimensions={1,2,3} | broadcast | bytes 10485760 | tf_op jit(solution)/shard_map/cond/branch_3_fun/tile | solution.py:621
  40.4 7.4 %all-to-all-start.1 = ((bf16[16,128,2048]{2,1,0:T(8,128)(2,1)}), bf16[16,128,2048]{2,1,0:T(8,128)(2,1)}, u32[]{:S(2)}, u32[]{:S(2)}) async-start(bf16[16,128,2048]{2,1,0:T(8,128)(2,1)} %bitcast.53), calls=%async_computation.1 | async-start | bytes 16777216 | tf_op jit(solution)/shard_map/cond/branch_3_fun/all_to_all | solution.py:622
  47.8 1.0 fusion.11
  48.8 3.4 %collective-permute-start.53 = (bf16[1,32,2048]{2,1,0:T(8,128)(2,1)S(1)}, bf16[1,32,2048]{2,1,0:T(8,128)(2,1)S(1)}, u32[]{:S(2)}, u32[]{:S(2)}) collective-permute-start(bf16[1,32,2048]{2,1,0:T(8,128)(2,1)S(1)} %get-tuple-element.480), channel_id=1, source_target_pairs={{0,1},{1,2},{2,3},{3,4},{4,5},{5,6},{6,7},{7,8},{8,9},{9,10},{10,1... | collective-permute-start | bytes 393224 | tf_op jit(solution)/shard_map/cond/branch_3_fun/ppermute | solution.py:614
  52.1 1.9 collective-permute-start.52
  54.1 0.3 copy.98
  55.1 0.7 copy.92
  55.8 0.6 slice.39
  56.4 0.7 copy.96.wide_w_ref
  57.1 0.8 convert_element_type.14.image_w_ref
  57.9 0.7 copy.97.pick_ref
  59.1 8.8 %spread_weights.1.spread_ref = bf16[16,256,144]{2,1,0:T(8,128)(2,1)} custom-call(f32[32,128]{1,0:T(8,128)} %copy.96.wide_w_ref, f32[32,16]{1,0:T(8,128)} %bitcast.64, f32[16,2,128]{2,1,0:T(2,128)} %copy.97.pick_ref, f32[16,1,16]{2,1,0:T(1,128)} %bitcast.66), custom_call_target="tpu_custom_call" | custom-call | tf_op jit(solution)/shard_map/cond/branch_3_fun/spread_weights/pallas_call | solution.py:276
  67.9 0.6 copy.108
  68.5 161.2 %collective-permute-done.53.rest_0_ = bf16[1,32,2048]{2,1,0:T(8,128)(2,1)S(1)} collective-permute-done((bf16[1,32,2048]{2,1,0:T(8,128)(2,1)S(1)}, bf16[1,32,2048]{2,1,0:T(8,128)(2,1)S(1)}, u32[]{:S(2)}, u32[]{:S(2)}) %collective-permute-start.53) | collective-permute-done | bytes 131104 | tf_op jit(solution)/shard_map/cond/branch_3_fun/ppermute | solution.py:614
  229.7 1.7 collective-permute-done.52.right_ref
  231.5 0.7 broadcast_in_dim.35.rest_2_
  232.1 2.2 broadcast_in_dim.9.coef_ref.rest_4_
  234.4 0.6 broadcast_6_table_ref.0.table_ref
  235.0 37.7 %slab_update.13 = (f32[128,32,2048]{2,1,0:T(8,128)}, bf16[16,2048]{1,0:T(8,128)(2,1)}) custom-call(s32[8,128]{1,0:T(8,128)} %broadcast_6_table_ref.0.table_ref, bf16[128,32,2048]{2,1,0:T(8,128)(2,1)} %get-tuple-element.328.lower_ref.upper_ref.next_ref, bf16[128,32,2048]{2,1,0:T(8,128)(2,1)} %get-tuple-element.328.lower_ref.upper_ref.next_ref, ...), custom_call_target="tpu_custom_call" | custom-call | flops 536870912 | bytes 58720256 | tf_op jit(solution)/shard_map/cond/branch_3_fun/slab_update/pallas_call | solution.py:185
  (43 shorter events, 1.2 us)
Async XLA Ops:
  0.0 6.9 %copy-start.28 = (s32[16]{0:T(128)S(1)}, s32[16]{0:T(128)}, u32[]{:S(2)}) copy-start(s32[16]{0:T(128)} %bases_ref.3) | copy-start | bytes 196
  0.0 11.0 %copy-start.13 = (bf16[16,32]{1,0:T(8,128)(2,1)S(1)}, bf16[16,32]{1,0:T(8,128)(2,1)}, u32[]{:S(2)}) copy-start(bf16[16,32]{1,0:T(8,128)(2,1)} %weight_ref.1) | copy-start | bytes 3076
  4.4 14.9 %collective-permute-start.54 = (bf16[64,2048]{1,0:T(8,128)(2,1)S(1)}, bf16[64,2048]{1,0:T(8,128)(2,1)}, u32[]{:S(2)}, u32[]{:S(2)}) collective-permute-start(bf16[64,2048]{1,0:T(8,128)(2,1)S(1)} %get-tuple-element.382), channel_id=1, source_target_pairs={{0,1},{1,0},{2,3},{3,2},{4,5},{5,4},{6,7},{7,6},{8,9},{9,8},{10,11... | collective-permute-start | bytes 786440 | tf_op jit(solution)/shard_map/ppermute | solution.py:634
  5.2 14.1 %collective-permute-start.55 = (bf16[64,2048]{1,0:T(8,128)(2,1)S(1)}, bf16[64,2048]{1,0:T(8,128)(2,1)}, u32[]{:S(2)}, u32[]{:S(2)}) collective-permute-start(bf16[64,2048]{1,0:T(8,128)(2,1)S(1)} %get-tuple-element.383), channel_id=1, source_target_pairs={{0,2},{1,3},{2,0},{3,1},{4,6},{5,7},{6,4},{7,5},{8,10},{9,11},{10,... | collective-permute-start | bytes 786440 | tf_op jit(solution)/shard_map/ppermute | solution.py:634
  5.4 14.9 %collective-permute-start.56 = (bf16[64,2048]{1,0:T(8,128)(2,1)S(1)}, bf16[64,2048]{1,0:T(8,128)(2,1)}, u32[]{:S(2)}, u32[]{:S(2)}) collective-permute-start(bf16[64,2048]{1,0:T(8,128)(2,1)S(1)} %get-tuple-element.384), channel_id=1, source_target_pairs={{0,3},{1,2},{2,1},{3,0},{4,7},{5,6},{6,5},{7,4},{8,11},{9,10},{10,... | collective-permute-start | bytes 786440 | tf_op jit(solution)/shard_map/ppermute | solution.py:634
  8.9 10.4 %collective-permute-start.57 = (bf16[1,32,2048]{2,1,0:T(8,128)(2,1)S(1)}, bf16[1,32,2048]{2,1,0:T(8,128)(2,1)}, u32[]{:S(2)}, u32[]{:S(2)}) collective-permute-start(bf16[1,32,2048]{2,1,0:T(8,128)(2,1)S(1)} %get-tuple-element.394), channel_id=1, source_target_pairs={{1,0},{2,1},{3,2},{4,3},{5,4},{6,5},{7,6},{8,7},{9,8},{10,9},{11,1... | collective-permute-start | bytes 393224 | tf_op jit(solution)/shard_map/ppermute | solution.py:651
  40.4 13.7 %copy-start.3 = (f32[16,2048]{1,0:T(8,128)S(1)}, f32[16,2048]{1,0:T(8,128)}, u32[]{:S(2)}) copy-start(f32[16,2048]{1,0:T(8,128)} %get-tuple-element.471) | copy-start | bytes 393220 | tf_op jit(solution)/shard_map/cond
  40.4 14.0 %copy-start.29 = (s32[16]{0:T(128)S(1)}, s32[16]{0:T(128)}, u32[]{:S(2)}) copy-start(s32[16]{0:T(128)} %get-tuple-element.332) | copy-start | bytes 196 | tf_op jit(solution)/shard_map/cond
  40.4 191.1 %all-to-all-start.1 = ((bf16[16,128,2048]{2,1,0:T(8,128)(2,1)}), bf16[16,128,2048]{2,1,0:T(8,128)(2,1)}, u32[]{:S(2)}, u32[]{:S(2)}) async-start(bf16[16,128,2048]{2,1,0:T(8,128)(2,1)} %bitcast.53), calls=%async_computation.1 | async-start | bytes 16777216 | tf_op jit(solution)/shard_map/cond/branch_3_fun/all_to_all | solution.py:622
  48.8 180.9 %collective-permute-start.53 = (bf16[1,32,2048]{2,1,0:T(8,128)(2,1)S(1)}, bf16[1,32,2048]{2,1,0:T(8,128)(2,1)S(1)}, u32[]{:S(2)}, u32[]{:S(2)}) collective-permute-start(bf16[1,32,2048]{2,1,0:T(8,128)(2,1)S(1)} %get-tuple-element.480), channel_id=1, source_target_pairs={{0,1},{1,2},{2,3},{3,4},{4,5},{5,6},{6,7},{7,8},{8,9},{9,10},{10,1... | collective-permute-start | bytes 393224 | tf_op jit(solution)/shard_map/cond/branch_3_fun/ppermute | solution.py:614
  52.1 179.3 %collective-permute-start.52 = (bf16[1,32,2048]{2,1,0:T(8,128)(2,1)S(1)}, bf16[1,32,2048]{2,1,0:T(8,128)(2,1)S(1)}, u32[]{:S(2)}, u32[]{:S(2)}) collective-permute-start(bf16[1,32,2048]{2,1,0:T(8,128)(2,1)S(1)} %get-tuple-element.481), channel_id=1, source_target_pairs={{1,0},{2,1},{3,2},{4,3},{5,4},{6,5},{7,6},{8,7},{9,8},{10,9},{11,1... | collective-permute-start | bytes 393224 | tf_op jit(solution)/shard_map/cond/branch_3_fun/ppermute | solution.py:615
  229.7 5.2 %copy-start.23 = (bf16[1,32,2048]{2,1,0:T(8,128)(2,1)}, bf16[1,32,2048]{2,1,0:T(8,128)(2,1)S(1)}, u32[]{:S(2)}) copy-start(bf16[1,32,2048]{2,1,0:T(8,128)(2,1)S(1)} %collective-permute-done.53.rest_0_) | copy-start | bytes 393220 | tf_op jit(solution)/shard_map/cond
  231.5 3.5 %copy-start.24 = (bf16[1,32,2048]{2,1,0:T(8,128)(2,1)}, bf16[1,32,2048]{2,1,0:T(8,128)(2,1)S(1)}, u32[]{:S(2)}) copy-start(bf16[1,32,2048]{2,1,0:T(8,128)(2,1)S(1)} %collective-permute-done.52.right_ref) | copy-start | bytes 393220 | tf_op jit(solution)/shard_map/cond
where the time goes:
time: 274 us; the launch traced here: 273 us
  waiting for transfers between devices  164 us (60%)
  Pallas kernels  60.7 us (22%)
  starting transfers between devices  17.2 us (6%)
  local copies, waits for them, and re-layouts  15.4 us (6%)
  blocking collectives  9.96 us (4%)
  other arithmetic  3.95 us (1%)
    ppermute x1, waiting for transfers between devices, dense(): left = lax.ppermute(volume[slices - 1:], 'slab', ups_of(1))  161 us
    pallas_call x1, Pallas kernels, update(): pl.pallas_call(functools.partial(update_kernel, dense, part), grid_spec=p...  37.7 us
    all_to_all x1, blocking collectives, dense(): lax.all_to_all(ends, 'slab', split_axis=0, concat_axis=0, tiled=True)  9.96 us
    pallas_call x2, Pallas kernels, turn(): pl.pallas_call(functools.partial(turn_kernel, classes, count, part), in_s...  8.97 us
    pallas_call x1, Pallas kernels, make_weights(): pl.pallas_call(weights_kernel, grid=(halves,), in_specs=[whole(wide_w), w...  8.81 us
    all_to_all x1, starting transfers between devices, dense(): lax.all_to_all(outgoing, 'slab', split_axis=0, concat_axis=0, tiled=True)  7.4 us
  transfers between devices with their start and end apart: 7, of which 3 were waited for; matrix products, arithmetic and copies ran while one was open for 2% of the time, Pallas kernels for 7%

commit v1 on v0

--- a/solution.py
+++ b/solution.py
@@ -530,7 +530,8 @@
     used = jnp.max(used, axis=0, keepdims=True)
     head = lane[:1]
     need = jnp.max(jnp.where(used >= 0, head + 1, 0))
-    need = jnp.where(jnp.max(to - at) > 0, slots * LOAD + 1, need)
+    left = jnp.max(jnp.where(lane < angles, to - at, 0))
+    need = jnp.where(left > 0, slots * LOAD + 1, need)
     which_ref[0] = sum(jnp.where(need > end, 1, 0) for end in ends)
 
     tall = -(-max(slots * LOAD, angles) // 8) * 8

time: 274 us -> 122 us (0.45)
  waiting for transfers between devices: 164 us -> 15.3 us
  starting transfers between devices: 17.2 us -> 32.1 us
  local copies, waits for them, and re-layouts: 15.4 us -> 1.41 us
  blocking collectives: 9.96 us -> 0 us
  Pallas kernels: 60.7 us -> 70.2 us
  other arithmetic: 3.95 us -> 0 us
    ppermute x2 -> x13, waiting for transfers between devices: 163 us -> 11.8 us  [the longest x6 8.33 us: branch(): other[part].append(lax.ppermute(go_other, 'slab', pairs[1]))]
    ppermute x2 -> x13, starting transfers between devices: 5.27 us -> 25.5 us  [the longest x6 20.5 us: branch(): other[part].append(lax.ppermute(go_other, 'slab', pairs[1]))]
    all_to_all x1 -> x0, blocking collectives: 9.96 us -> none  [dense(): lax.all_to_all(ends, 'slab', split_axis=0, concat_axis=0, tiled=True)]
    pallas_call x1 -> x7, Pallas kernels: 8.81 us -> 18.2 us  [the longest x6 16.2 us: choose(): pl.pallas_call(functools.partial(choose_kernel, slot, part, load, len(own...]
    pallas_call x1 -> x4, Pallas kernels: 3.15 us -> 11.4 us  [device_tables(): pl.pallas_call(functools.partial(tables_kernel, rows, part * blocks + her...]
    pallas_call x1 -> x2, Pallas kernels: 37.7 us -> 29.5 us  [update(): pl.pallas_call(functools.partial(update_kernel, dense, part), grid_spec=p...]
    all_to_all x1 -> x0, starting transfers between devices: 7.4 us -> none  [dense(): lax.all_to_all(outgoing, 'slab', split_axis=0, concat_axis=0, tiled=True)]
    another operation x8 -> x0, local copies, waits for them, and re-layouts: 5.65 us -> none  [the longest x1 4.46 us: dense(): jnp.tile(by_class, (planes, 1, 1, 1)).reshape(angles, slices, cols)]
  transfers between devices with their start and end apart: 7 -> 20, of which waited for: 3 -> 9; matrix products, arithmetic and copies ran while one was open for 2% -> 0% of each run, Pallas kernels for 7% -> 53%
where the time goes in v1:
time: 122 us; the launch traced here: 120 us
  Pallas kernels  70.2 us (58%)
  starting transfers between devices  32.1 us (26%)
  waiting for transfers between devices  15.3 us (13%)
  local copies, waits for them, and re-layouts  1.41 us (1%)
    pallas_call x2, Pallas kernels, update(): pl.pallas_call(functools.partial(update_kernel, dense, part), grid_spec=p...  29.5 us
    ppermute x6, starting transfers between devices, branch(): other[part].append(lax.ppermute(go_other, 'slab', pairs[1]))  20.5 us
    pallas_call x6, Pallas kernels, choose(): pl.pallas_call(functools.partial(choose_kernel, slot, part, load, len(own...  16.2 us
    pallas_call x4, Pallas kernels, device_tables(): pl.pallas_call(functools.partial(tables_kernel, rows, part * blocks + her...  11.4 us
    pallas_call x2, Pallas kernels, turn(): pl.pallas_call(functools.partial(turn_kernel, classes, count, part), in_s...  8.97 us
    ppermute x6, waiting for transfers between devices, branch(): other[part].append(lax.ppermute(go_other, 'slab', pairs[1]))  8.33 us
    ppermute x6, starting transfers between devices, on_device(): lax.ppermute(runs[d], 'slab', [(i, i ^ d) for i in range(nslab)])  4.59 us
    ppermute x1, starting transfers between devices, branch(): ahead = lax.ppermute(last, 'slab', ups_of(1))  4.29 us
  transfers between devices with their start and end apart: 20, of which 9 were waited for; matrix products, arithmetic and copies ran while one was open for 0% of the time, Pallas kernels for 53%

profile of v1, /device:TPU:15, one launch (start us, length us, event | category | flops | bytes accessed | tf_op | source)
XLA Modules:
  0.0 120.1 jit_solution(11253935627551708278)
XLA Ops:
  0.0 4.4 %turn_rows.2 = (bf16[64,2048]{1,0:T(8,128)(2,1)}, bf16[64,2048]{1,0:T(8,128)(2,1)S(1)}, bf16[64,2048]{1,0:T(8,128)(2,1)S(1)}, bf16[64,2048]{1,0:T(8,128)(2,1)S(1)}, bf16[1,32,2048]{2,1,0:T(8,128)(2,1)S(1)}) custom-call(s32[1]{0:T(128)} %bitcast.24.device_ref, s32[16]{0:T(128)} %bases_ref.3, bf16[512,2048]{1,0:T(8,128)(2,1)} %bitcast.54, ...), custom_call_target="tpu_custom_call" | custom-call | tf_op jit(solution)/shard_map/turn_rows/pallas_call | solution.py:473
  5.4 1.4 %collective-permute-start.56 = (bf16[64,2048]{1,0:T(8,128)(2,1)S(1)}, bf16[64,2048]{1,0:T(8,128)(2,1)}, u32[]{:S(2)}, u32[]{:S(2)}) collective-permute-start(bf16[64,2048]{1,0:T(8,128)(2,1)S(1)} %get-tuple-element.384), channel_id=1, source_target_pairs={{0,3},{1,2},{2,1},{3,0},{4,7},{5,6},{6,5},{7,4},{8,11},{9,10},{10,... | collective-permute-start | bytes 786440 | tf_op jit(solution)/shard_map/ppermute | solution.py:635
  6.9 2.0 %plan_slots.1 = (s32[16,128]{1,0:T(8,128)S(1)}, s32[1]{0:T(128)}) custom-call(s32[1]{0:T(128)} %bitcast.24.device_ref, s32[1,128]{1,0:T(1,128)S(1)} %pad_bitcast_fusion.1.bases_ref), custom_call_target="tpu_custom_call" | custom-call | tf_op jit(solution)/shard_map/plan_slots/pallas_call | solution.py:644
  8.9 2.1 %collective-permute-start.57 = (bf16[1,32,2048]{2,1,0:T(8,128)(2,1)S(1)}, bf16[1,32,2048]{2,1,0:T(8,128)(2,1)}, u32[]{:S(2)}, u32[]{:S(2)}) collective-permute-start(bf16[1,32,2048]{2,1,0:T(8,128)(2,1)S(1)} %get-tuple-element.394), channel_id=1, source_target_pairs={{1,0},{2,1},{3,2},{4,3},{5,4},{6,5},{7,6},{8,7},{9,8},{10,9},{11,1... | collective-permute-start | bytes 393224 | tf_op jit(solution)/shard_map/ppermute | solution.py:652
  11.0 3.2 %make_tables.19 = (f32[4,2,3,128,128]{4,3,2,1,0:T(8,128)S(1)}, bf16[8,256,144]{2,1,0:T(8,128)(2,1)S(1)}, bf16[128,256]{1,0:T(8,128)(2,1)}) custom-call(s32[1]{0:T(128)} %bitcast.24.device_ref, s32[1,128]{1,0:T(1,128)S(1)} %pad_bitcast_fusion.1.bases_ref, f32[16,2048]{1,0:T(8,128)} %after_ref.1, f32[16,2048]{1,0:T(8,128)} %after_ref.1, ...), custom_call_target="tpu_custom_call" | custom-call | tf_op jit(solution)/shard_map/make_tables/pallas_call | solution.py:414
  14.2 4.6 %turn_rows.3 = (bf16[64,2048]{1,0:T(8,128)(2,1)}, bf16[64,2048]{1,0:T(8,128)(2,1)}, bf16[64,2048]{1,0:T(8,128)(2,1)}, bf16[64,2048]{1,0:T(8,128)(2,1)}, bf16[1,32,2048]{2,1,0:T(8,128)(2,1)}) custom-call(s32[1]{0:T(128)} %bitcast.24.device_ref, s32[16]{0:T(128)} %bases_ref.3, bf16[512,2048]{1,0:T(8,128)(2,1)} %bitcast.55, bf16[128,32,2048]{2,1,0:T(8,128)(2,1)} %volume_ref.3), custom_call_target="tpu_custom_call" | custom-call | tf_op jit(solution)/shard_map/turn_rows/pallas_call | solution.py:473
  20.3 99.7 %conditional.1 = (f32[128,32,2048]{2,1,0:T(8,128)}) conditional(s32[]{:T(128)} %bitcast.27, (s32[16,128]{1,0:T(8,128)S(1)}, bf16[64,2048]{1,0:T(8,128)(2,1)}, bf16[64,2048]{1,0:T(8,128)(2,1)}, bf16[64,2048]{1,0:T(8,128)(2,1)}, bf16[64,2048]{1,0:T(8,128)(2,1)}, /*index=5*/s32[1,128]{1,0:T(1,128)S(1)}, s32[1]{0:T(128)}, ...), branch_computations={%region_0.1_spmd, %region_1.2_spmd, %region_2.3_spmd, %region_3.5_... | conditional | flops 541218752 | bytes 112460800 | solution.py:686
  21.0 1.5 %collective-permute-start.4 = (bf16[64,2048]{1,0:T(8,128)(2,1)}, bf16[64,2048]{1,0:T(8,128)(2,1)}, u32[]{:S(2)}, u32[]{:S(2)}) collective-permute-start(bf16[64,2048]{1,0:T(8,128)(2,1)} %get-tuple-element.162), channel_id=1, source_target_pairs={{0,3},{1,2},{2,1},{3,0},{4,7},{5,6},{6,5},{7,4},{8,11},{9,10},{10,... | collective-permute-start | bytes 786440 | tf_op jit(solution)/shard_map/cond/branch_0_fun/ppermute | solution.py:635
  22.5 2.9 %choose_packet.20 = (bf16[2,64,2048]{2,1,0:T(8,128)(2,1)}, bf16[2,64,2048]{2,1,0:T(8,128)(2,1)}) custom-call(s32[16,128]{1,0:T(8,128)S(1)} %get-tuple-element.175.table_ref, bf16[64,2048]{1,0:T(8,128)(2,1)} %get-tuple-element.134.refs_0_.rest_0_, bf16[64,2048]{1,0:T(8,128)(2,1)} %get-tuple-element.135.refs_1_.rest_1_, ...), custom_call_target="tpu_custom_call" | custom-call | bytes 2097152 | tf_op jit(solution)/shard_map/cond/branch_0_fun/choose_packet/pallas_call | solution.py:586
  25.7 4.0 %collective-permute-start.1 = (bf16[2,64,2048]{2,1,0:T(8,128)(2,1)}, bf16[2,64,2048]{2,1,0:T(8,128)(2,1)}, u32[]{:S(2)}, u32[]{:S(2)}) collective-permute-start(bf16[2,64,2048]{2,1,0:T(8,128)(2,1)} %get-tuple-element.151), channel_id=1, source_target_pairs={{4,8},{5,9},{6,10},{7,11},{8,4},{9,5},{10,6},{11,7},{20,24},{21,25... | collective-permute-start | bytes 1572872 | tf_op jit(solution)/shard_map/cond/branch_0_fun/ppermute | solution.py:676
  29.7 2.6 %make_tables.10 = (f32[4,2,3,128,128]{4,3,2,1,0:T(8,128)S(1)}, bf16[8,256,144]{2,1,0:T(8,128)(2,1)S(1)}) custom-call(s32[1]{0:T(128)} %get-tuple-element.132.device_ref, s32[1,128]{1,0:T(1,128)S(1)} %get-tuple-element.167.bases_ref, f32[16,2048]{1,0:T(8,128)} %get-tuple-element.142.own_ref.after_ref, ...), custom_call_target="tpu_custom_call", output_to_operand_aliasing={{0}: (5, {}), {1}: (6, {})} | custom-call | tf_op jit(solution)/shard_map/cond/branch_0_fun/make_tables/pallas_call | solution.py:414
  32.3 2.5 %collective-permute-done.4.refs_3_.rest_3_ = bf16[64,2048]{1,0:T(8,128)(2,1)} collective-permute-done((bf16[64,2048]{1,0:T(8,128)(2,1)}, bf16[64,2048]{1,0:T(8,128)(2,1)}, u32[]{:S(2)}, u32[]{:S(2)}) %collective-permute-start.4) | collective-permute-done | bytes 262176 | tf_op jit(solution)/shard_map/cond/branch_0_fun/ppermute | solution.py:635
  34.8 2.8 %choose_packet.22 = (bf16[2,64,2048]{2,1,0:T(8,128)(2,1)}, bf16[2,64,2048]{2,1,0:T(8,128)(2,1)}) custom-call(s32[16,128]{1,0:T(8,128)S(1)} %get-tuple-element.175.table_ref, bf16[64,2048]{1,0:T(8,128)(2,1)S(1)} %copy-done.7, bf16[64,2048]{1,0:T(8,128)(2,1)} %copy-done.11, bf16[64,2048]{1,0:T(8,128)(2,1)} %collective-permute-done.3.refs_2_.rest_2_, ...), custom_call_target="tpu_custom_call" | custom-call | bytes 2097152 | tf_op jit(solution)/shard_map/cond/branch_0_fun/choose_packet/pallas_call | solution.py:586
  37.8 4.0 %collective-permute-start.6 = (bf16[2,64,2048]{2,1,0:T(8,128)(2,1)}, bf16[2,64,2048]{2,1,0:T(8,128)(2,1)}, u32[]{:S(2)}, u32[]{:S(2)}) collective-permute-start(bf16[2,64,2048]{2,1,0:T(8,128)(2,1)} %get-tuple-element.164), channel_id=1, source_target_pairs={{4,8},{5,9},{6,10},{7,11},{8,4},{9,5},{10,6},{11,7},{20,24},{21,25... | collective-permute-start | bytes 1572872 | tf_op jit(solution)/shard_map/cond/branch_0_fun/ppermute | solution.py:676
  42.2 2.8 %choose_packet.21 = (bf16[2,64,2048]{2,1,0:T(8,128)(2,1)}, bf16[2,64,2048]{2,1,0:T(8,128)(2,1)}) custom-call(s32[16,128]{1,0:T(8,128)S(1)} %get-tuple-element.175.table_ref, bf16[64,2048]{1,0:T(8,128)(2,1)S(1)} %copy-done.4, bf16[64,2048]{1,0:T(8,128)(2,1)} %get-tuple-element.135.refs_1_.rest_1_, bf16[64,2048]{1,0:T(8,128)(2,1)} %get-tuple-element.136.refs_2_.rest_2_, ...), custom_call_target="tpu_custom_call" | custom-call | bytes 2097152 | tf_op jit(solution)/shard_map/cond/branch_0_fun/choose_packet/pallas_call | solution.py:586
  45.2 3.2 %collective-permute-start.8 = (bf16[2,64,2048]{2,1,0:T(8,128)(2,1)}, bf16[2,64,2048]{2,1,0:T(8,128)(2,1)}, u32[]{:S(2)}, u32[]{:S(2)}) collective-permute-start(bf16[2,64,2048]{2,1,0:T(8,128)(2,1)} %get-tuple-element.182), channel_id=1, source_target_pairs={{4,8},{5,9},{6,10},{7,11},{8,4},{9,5},{10,6},{11,7},{20,24},{21,25... | collective-permute-start | bytes 1572872 | tf_op jit(solution)/shard_map/cond/branch_0_fun/ppermute | solution.py:676
  48.3 3.1 %make_tables.11 = (f32[4,2,3,128,128]{4,3,2,1,0:T(8,128)}, bf16[8,256,144]{2,1,0:T(8,128)(2,1)}, bf16[128,256]{1,0:T(8,128)(2,1)}) custom-call(s32[1]{0:T(128)} %get-tuple-element.132.device_ref, s32[1,128]{1,0:T(1,128)S(1)} %get-tuple-element.167.bases_ref, f32[16,2048]{1,0:T(8,128)S(1)} %copy-done, f32[16,2048]{1,0:T(8,128)S(1)} %copy-done, ...), custom_call_target="tpu_custom_call" | custom-call | tf_op jit(solution)/shard_map/cond/branch_0_fun/make_tables/pallas_call | solution.py:414
  51.9 2.6 %collective-permute-done.6.refs_5_.refs_6_.rest_7_ = bf16[2,64,2048]{2,1,0:T(8,128)(2,1)} collective-permute-done((bf16[2,64,2048]{2,1,0:T(8,128)(2,1)}, bf16[2,64,2048]{2,1,0:T(8,128)(2,1)}, u32[]{:S(2)}, u32[]{:S(2)}) %collective-permute-start.6) | collective-permute-done | bytes 524320 | tf_op jit(solution)/shard_map/cond/branch_0_fun/ppermute | solution.py:676
  54.5 2.8 %choose_packet.23 = (bf16[2,64,2048]{2,1,0:T(8,128)(2,1)}, bf16[2,64,2048]{2,1,0:T(8,128)(2,1)}) custom-call(s32[16,128]{1,0:T(8,128)S(1)} %get-tuple-element.175.table_ref, bf16[64,2048]{1,0:T(8,128)(2,1)S(1)} %copy-done.7, bf16[64,2048]{1,0:T(8,128)(2,1)} %copy-done.11, bf16[64,2048]{1,0:T(8,128)(2,1)} %collective-permute-done.3.refs_2_.rest_2_, ...), custom_call_target="tpu_custom_call" | custom-call | bytes 2097152 | tf_op jit(solution)/shard_map/cond/branch_0_fun/choose_packet/pallas_call | solution.py:586
  57.4 3.1 %collective-permute-start.13 = (bf16[2,64,2048]{2,1,0:T(8,128)(2,1)}, bf16[2,64,2048]{2,1,0:T(8,128)(2,1)}, u32[]{:S(2)}, u32[]{:S(2)}) collective-permute-start(bf16[2,64,2048]{2,1,0:T(8,128)(2,1)} %get-tuple-element.190), channel_id=1, source_target_pairs={{4,8},{5,9},{6,10},{7,11},{8,4},{9,5},{10,6},{11,7},{20,24},{21,25... | collective-permute-start | bytes 1572872 | tf_op jit(solution)/shard_map/cond/branch_0_fun/ppermute | solution.py:676
  60.5 2.6 %make_tables.12 = (f32[4,2,3,128,128]{4,3,2,1,0:T(8,128)}, bf16[8,256,144]{2,1,0:T(8,128)(2,1)}) custom-call(s32[1]{0:T(128)} %get-tuple-element.132.device_ref, s32[1,128]{1,0:T(1,128)S(1)} %get-tuple-element.167.bases_ref, f32[16,2048]{1,0:T(8,128)S(1)} %copy-done, f32[16,2048]{1,0:T(8,128)S(1)} %copy-done, ...), custom_call_target="tpu_custom_call", output_to_operand_aliasing={{0}: (5, {}), {1}: (6, {})} | custom-call | tf_op jit(solution)/shard_map/cond/branch_0_fun/make_tables/pallas_call | solution.py:414
  63.1 2.6 %collective-permute-done.8.refs_7_.rest_8_ = bf16[2,64,2048]{2,1,0:T(8,128)(2,1)} collective-permute-done((bf16[2,64,2048]{2,1,0:T(8,128)(2,1)}, bf16[2,64,2048]{2,1,0:T(8,128)(2,1)}, u32[]{:S(2)}, u32[]{:S(2)}) %collective-permute-start.8) | collective-permute-done | bytes 524320 | tf_op jit(solution)/shard_map/cond/branch_0_fun/ppermute | solution.py:676
  65.8 2.4 %choose_packet.24 = (bf16[1,64,2048]{2,1,0:T(8,128)(2,1)}, bf16[1,64,2048]{2,1,0:T(8,128)(2,1)}) custom-call(s32[16,128]{1,0:T(8,128)S(1)} %get-tuple-element.175.table_ref, bf16[64,2048]{1,0:T(8,128)(2,1)S(1)} %copy-done.4, bf16[64,2048]{1,0:T(8,128)(2,1)} %get-tuple-element.135.refs_1_.rest_1_, bf16[64,2048]{1,0:T(8,128)(2,1)} %get-tuple-element.136.refs_2_.rest_2_, ...), custom_call_target="tpu_custom_call" | custom-call | bytes 1048576 | tf_op jit(solution)/shard_map/cond/branch_0_fun/choose_packet/pallas_call | solution.py:586
  68.3 3.1 %collective-permute-start.10 = (bf16[1,64,2048]{2,1,0:T(8,128)(2,1)}, bf16[1,64,2048]{2,1,0:T(8,128)(2,1)}, u32[]{:S(2)}, u32[]{:S(2)}) collective-permute-start(bf16[1,64,2048]{2,1,0:T(8,128)(2,1)} %get-tuple-element.184), channel_id=1, source_target_pairs={{4,8},{5,9},{6,10},{7,11},{8,4},{9,5},{10,6},{11,7},{20,24},{21,25... | collective-permute-start | bytes 786440 | tf_op jit(solution)/shard_map/cond/branch_0_fun/ppermute | solution.py:676
  71.4 2.9 %collective-permute-done.12.refs_5_.rest_5_ = bf16[2,64,2048]{2,1,0:T(8,128)(2,1)} collective-permute-done((bf16[2,64,2048]{2,1,0:T(8,128)(2,1)}, bf16[2,64,2048]{2,1,0:T(8,128)(2,1)}, u32[]{:S(2)}, u32[]{:S(2)}) %collective-permute-start.12) | collective-permute-done | bytes 524320 | tf_op jit(solution)/shard_map/cond/branch_0_fun/ppermute | solution.py:675
  74.4 2.6 %collective-permute-done.13.refs_7_.rest_8_ = bf16[2,64,2048]{2,1,0:T(8,128)(2,1)} collective-permute-done((bf16[2,64,2048]{2,1,0:T(8,128)(2,1)}, bf16[2,64,2048]{2,1,0:T(8,128)(2,1)}, u32[]{:S(2)}, u32[]{:S(2)}) %collective-permute-start.13) | collective-permute-done | bytes 524320 | tf_op jit(solution)/shard_map/cond/branch_0_fun/ppermute | solution.py:676
  77.0 2.4 %choose_packet.25 = (bf16[1,64,2048]{2,1,0:T(8,128)(2,1)}, bf16[1,64,2048]{2,1,0:T(8,128)(2,1)}) custom-call(s32[16,128]{1,0:T(8,128)S(1)} %get-tuple-element.175.table_ref, bf16[64,2048]{1,0:T(8,128)(2,1)S(1)} %copy-done.7, bf16[64,2048]{1,0:T(8,128)(2,1)} %copy-done.11, bf16[64,2048]{1,0:T(8,128)(2,1)} %collective-permute-done.3.refs_2_.rest_2_, ...), custom_call_target="tpu_custom_call" | custom-call | bytes 1048576 | tf_op jit(solution)/shard_map/cond/branch_0_fun/choose_packet/pallas_call | solution.py:586
  79.5 3.1 %collective-permute-start.15 = (bf16[1,64,2048]{2,1,0:T(8,128)(2,1)}, bf16[1,64,2048]{2,1,0:T(8,128)(2,1)S(1)}, u32[]{:S(2)}, u32[]{:S(2)}) collective-permute-start(bf16[1,64,2048]{2,1,0:T(8,128)(2,1)} %get-tuple-element.192), channel_id=1, source_target_pairs={{4,8},{5,9},{6,10},{7,11},{8,4},{9,5},{10,6},{11,7},{20,24},{21,25... | collective-permute-start | bytes 786440 | tf_op jit(solution)/shard_map/cond/branch_0_fun/ppermute | solution.py:676
  82.7 14.3 %slab_update.7 = (f32[128,32,2048]{2,1,0:T(8,128)}, bf16[16,2048]{1,0:T(8,128)(2,1)}) custom-call(s32[16,128]{1,0:T(8,128)S(1)} %get-tuple-element.175.table_ref, bf16[128,32,2048]{2,1,0:T(8,128)(2,1)} %get-tuple-element.176.lower_ref.upper_ref.next_ref, bf16[128,32,2048]{2,1,0:T(8,128)(2,1)} %get-tuple-element.176.lower_ref.upper_ref.next_ref, ...), custom_call_target="tpu_custom_call" | custom-call | flops 268435456 | bytes 29360128 | tf_op jit(solution)/shard_map/cond/branch_0_fun/slab_update/pallas_call | solution.py:185
  97.0 4.3 %collective-permute-start.11 = (bf16[16,2048]{1,0:T(8,128)(2,1)}, bf16[16,2048]{1,0:T(8,128)(2,1)S(1)}, u32[]{:S(2)}, u32[]{:S(2)}) collective-permute-start(bf16[16,2048]{1,0:T(8,128)(2,1)} %get-tuple-element.185), channel_id=1, source_target_pairs={{0,1},{1,2},{2,3},{3,4},{4,5},{5,6},{6,7},{7,8},{8,9},{9,10},{10,1... | collective-permute-start | bytes 196616 | tf_op jit(solution)/shard_map/cond/branch_0_fun/ppermute | solution.py:679
  102.1 15.3 %slab_update.8 = (f32[128,32,2048]{2,1,0:T(8,128)}, bf16[16,2048]{1,0:T(8,128)(2,1)}) custom-call(s32[16,128]{1,0:T(8,128)S(1)} %get-tuple-element.175.table_ref, bf16[128,32,2048]{2,1,0:T(8,128)(2,1)} %get-tuple-element.176.lower_ref.upper_ref.next_ref, ...), custom_call_target="tpu_custom_call", output_to_operand_aliasing={{0}: (19, {})} | custom-call | flops 268435456 | bytes 29360128 | tf_op jit(solution)/shard_map/cond/branch_0_fun/slab_update/pallas_call | solution.py:185
  118.0 2.0 %mend_slices.3 = f32[128,32,2048]{2,1,0:T(8,128)} custom-call(bf16[8,256,144]{2,1,0:T(8,128)(2,1)} %get-tuple-element.173.spread_ref.lower_ref, bf16[8,256,144]{2,1,0:T(8,128)(2,1)S(1)} %get-tuple-element.174.spread_ref.upper_ref, bf16[16,2048]{1,0:T(8,128)(2,1)} %copy-done.26, ...), custom_call_target="tpu_custom_call", output_to_operand_aliasing={{}: (4, {})} | custom-call | tf_op jit(solution)/shard_map/cond/branch_0_fun/mend_slices/pallas_call | solution.py:236
  (46 shorter events, 5.8 us)
Async XLA Ops:
  0.0 6.9 %copy-start.28 = (s32[16]{0:T(128)S(1)}, s32[16]{0:T(128)}, u32[]{:S(2)}) copy-start(s32[16]{0:T(128)} %bases_ref.3) | copy-start | bytes 196
  0.0 11.0 %copy-start.13 = (bf16[16,32]{1,0:T(8,128)(2,1)S(1)}, bf16[16,32]{1,0:T(8,128)(2,1)}, u32[]{:S(2)}) copy-start(bf16[16,32]{1,0:T(8,128)(2,1)} %weight_ref.1) | copy-start | bytes 3076
  4.4 14.9 %collective-permute-start.54 = (bf16[64,2048]{1,0:T(8,128)(2,1)S(1)}, bf16[64,2048]{1,0:T(8,128)(2,1)}, u32[]{:S(2)}, u32[]{:S(2)}) collective-permute-start(bf16[64,2048]{1,0:T(8,128)(2,1)S(1)} %get-tuple-element.382), channel_id=1, source_target_pairs={{0,1},{1,0},{2,3},{3,2},{4,5},{5,4},{6,7},{7,6},{8,9},{9,8},{10,11... | collective-permute-start | bytes 786440 | tf_op jit(solution)/shard_map/ppermute | solution.py:635
  5.2 14.1 %collective-permute-start.55 = (bf16[64,2048]{1,0:T(8,128)(2,1)S(1)}, bf16[64,2048]{1,0:T(8,128)(2,1)}, u32[]{:S(2)}, u32[]{:S(2)}) collective-permute-start(bf16[64,2048]{1,0:T(8,128)(2,1)S(1)} %get-tuple-element.383), channel_id=1, source_target_pairs={{0,2},{1,3},{2,0},{3,1},{4,6},{5,7},{6,4},{7,5},{8,10},{9,11},{10,... | collective-permute-start | bytes 786440 | tf_op jit(solution)/shard_map/ppermute | solution.py:635
  5.4 14.9 %collective-permute-start.56 = (bf16[64,2048]{1,0:T(8,128)(2,1)S(1)}, bf16[64,2048]{1,0:T(8,128)(2,1)}, u32[]{:S(2)}, u32[]{:S(2)}) collective-permute-start(bf16[64,2048]{1,0:T(8,128)(2,1)S(1)} %get-tuple-element.384), channel_id=1, source_target_pairs={{0,3},{1,2},{2,1},{3,0},{4,7},{5,6},{6,5},{7,4},{8,11},{9,10},{10,... | collective-permute-start | bytes 786440 | tf_op jit(solution)/shard_map/ppermute | solution.py:635
  8.9 10.4 %collective-permute-start.57 = (bf16[1,32,2048]{2,1,0:T(8,128)(2,1)S(1)}, bf16[1,32,2048]{2,1,0:T(8,128)(2,1)}, u32[]{:S(2)}, u32[]{:S(2)}) collective-permute-start(bf16[1,32,2048]{2,1,0:T(8,128)(2,1)S(1)} %get-tuple-element.394), channel_id=1, source_target_pairs={{1,0},{2,1},{3,2},{4,3},{5,4},{6,5},{7,6},{8,7},{9,8},{10,9},{11,1... | collective-permute-start | bytes 393224 | tf_op jit(solution)/shard_map/ppermute | solution.py:652
  20.3 14.5 %copy-start.7 = (bf16[64,2048]{1,0:T(8,128)(2,1)S(1)}, bf16[64,2048]{1,0:T(8,128)(2,1)}, u32[]{:S(2)}) copy-start(bf16[64,2048]{1,0:T(8,128)(2,1)} %get-tuple-element.159.refs_0_.rest_0_) | copy-start | bytes 786436 | tf_op jit(solution)/shard_map/cond
  20.3 12.0 %collective-permute-start.2 = (bf16[64,2048]{1,0:T(8,128)(2,1)}, bf16[64,2048]{1,0:T(8,128)(2,1)S(1)}, u32[]{:S(2)}, u32[]{:S(2)}) collective-permute-start(bf16[64,2048]{1,0:T(8,128)(2,1)} %get-tuple-element.160), channel_id=1, source_target_pairs={{0,1},{1,0},{2,3},{3,2},{4,5},{5,4},{6,7},{7,6},{8,9},{9,8},{10,11... | collective-permute-start | bytes 786440 | tf_op jit(solution)/shard_map/cond/branch_0_fun/ppermute | solution.py:635
  20.6 11.7 %collective-permute-start.3 = (bf16[64,2048]{1,0:T(8,128)(2,1)}, bf16[64,2048]{1,0:T(8,128)(2,1)}, u32[]{:S(2)}, u32[]{:S(2)}) collective-permute-start(bf16[64,2048]{1,0:T(8,128)(2,1)} %get-tuple-element.161), channel_id=1, source_target_pairs={{0,2},{1,3},{2,0},{3,1},{4,6},{5,7},{6,4},{7,5},{8,10},{9,11},{10,... | collective-permute-start | bytes 786440 | tf_op jit(solution)/shard_map/cond/branch_0_fun/ppermute | solution.py:635
  21.0 13.8 %collective-permute-start.4 = (bf16[64,2048]{1,0:T(8,128)(2,1)}, bf16[64,2048]{1,0:T(8,128)(2,1)}, u32[]{:S(2)}, u32[]{:S(2)}) collective-permute-start(bf16[64,2048]{1,0:T(8,128)(2,1)} %get-tuple-element.162), channel_id=1, source_target_pairs={{0,3},{1,2},{2,1},{3,0},{4,7},{5,6},{6,5},{7,4},{8,11},{9,10},{10,... | collective-permute-start | bytes 786440 | tf_op jit(solution)/shard_map/cond/branch_0_fun/ppermute | solution.py:635
  25.4 16.9 %copy-start.4 = (bf16[64,2048]{1,0:T(8,128)(2,1)S(1)}, bf16[64,2048]{1,0:T(8,128)(2,1)}, u32[]{:S(2)}) copy-start(bf16[64,2048]{1,0:T(8,128)(2,1)} %get-tuple-element.134.refs_0_.rest_0_) | copy-start | bytes 786436 | tf_op jit(solution)/shard_map/cond
  25.4 16.4 %collective-permute-start = (bf16[2,64,2048]{2,1,0:T(8,128)(2,1)}, bf16[2,64,2048]{2,1,0:T(8,128)(2,1)}, u32[]{:S(2)}, u32[]{:S(2)}) collective-permute-start(bf16[2,64,2048]{2,1,0:T(8,128)(2,1)} %get-tuple-element.150), channel_id=1, source_target_pairs={{0,4},{1,5},{2,6},{3,7},{8,12},{9,13},{10,14},{11,15},{4,0},{5,1},... | collective-permute-start | bytes 1572872 | tf_op jit(solution)/shard_map/cond/branch_0_fun/ppermute | solution.py:675
  25.7 16.5 %collective-permute-start.1 = (bf16[2,64,2048]{2,1,0:T(8,128)(2,1)}, bf16[2,64,2048]{2,1,0:T(8,128)(2,1)}, u32[]{:S(2)}, u32[]{:S(2)}) collective-permute-start(bf16[2,64,2048]{2,1,0:T(8,128)(2,1)} %get-tuple-element.151), channel_id=1, source_target_pairs={{4,8},{5,9},{6,10},{7,11},{8,4},{9,5},{10,6},{11,7},{20,24},{21,25... | collective-permute-start | bytes 1572872 | tf_op jit(solution)/shard_map/cond/branch_0_fun/ppermute | solution.py:676
  32.3 16.1 %copy-start = (f32[16,2048]{1,0:T(8,128)S(1)}, f32[16,2048]{1,0:T(8,128)}, u32[]{:S(2)}) copy-start(f32[16,2048]{1,0:T(8,128)} %get-tuple-element.142.own_ref.after_ref) | copy-start | bytes 393220 | tf_op jit(solution)/shard_map/cond
  32.3 2.5 %copy-start.11 = (bf16[64,2048]{1,0:T(8,128)(2,1)}, bf16[64,2048]{1,0:T(8,128)(2,1)S(1)}, u32[]{:S(2)}) copy-start(bf16[64,2048]{1,0:T(8,128)(2,1)S(1)} %collective-permute-done.2.refs_1_.rest_1_) | copy-start | bytes 786436 | tf_op jit(solution)/shard_map/cond
  37.7 14.2 %collective-permute-start.5 = (bf16[2,64,2048]{2,1,0:T(8,128)(2,1)}, bf16[2,64,2048]{2,1,0:T(8,128)(2,1)}, u32[]{:S(2)}, u32[]{:S(2)}) collective-permute-start(bf16[2,64,2048]{2,1,0:T(8,128)(2,1)} %get-tuple-element.163), channel_id=1, source_target_pairs={{0,4},{1,5},{2,6},{3,7},{8,12},{9,13},{10,14},{11,15},{4,0},{5,1},... | collective-permute-start | bytes 1572872 | tf_op jit(solution)/shard_map/cond/branch_0_fun/ppermute | solution.py:675
  37.8 16.8 %collective-permute-start.6 = (bf16[2,64,2048]{2,1,0:T(8,128)(2,1)}, bf16[2,64,2048]{2,1,0:T(8,128)(2,1)}, u32[]{:S(2)}, u32[]{:S(2)}) collective-permute-start(bf16[2,64,2048]{2,1,0:T(8,128)(2,1)} %get-tuple-element.164), channel_id=1, source_target_pairs={{4,8},{5,9},{6,10},{7,11},{8,4},{9,5},{10,6},{11,7},{20,24},{21,25... | collective-permute-start | bytes 1572872 | tf_op jit(solution)/shard_map/cond/branch_0_fun/ppermute | solution.py:676
  45.1 18.1 %collective-permute-start.7 = (bf16[2,64,2048]{2,1,0:T(8,128)(2,1)}, bf16[2,64,2048]{2,1,0:T(8,128)(2,1)}, u32[]{:S(2)}, u32[]{:S(2)}) collective-permute-start(bf16[2,64,2048]{2,1,0:T(8,128)(2,1)} %get-tuple-element.181), channel_id=1, source_target_pairs={{0,4},{1,5},{2,6},{3,7},{8,12},{9,13},{10,14},{11,15},{4,0},{5,1},... | collective-permute-start | bytes 1572872 | tf_op jit(solution)/shard_map/cond/branch_0_fun/ppermute | solution.py:675
  45.2 20.6 %collective-permute-start.8 = (bf16[2,64,2048]{2,1,0:T(8,128)(2,1)}, bf16[2,64,2048]{2,1,0:T(8,128)(2,1)}, u32[]{:S(2)}, u32[]{:S(2)}) collective-permute-start(bf16[2,64,2048]{2,1,0:T(8,128)(2,1)} %get-tuple-element.182), channel_id=1, source_target_pairs={{4,8},{5,9},{6,10},{7,11},{8,4},{9,5},{10,6},{11,7},{20,24},{21,25... | collective-permute-start | bytes 1572872 | tf_op jit(solution)/shard_map/cond/branch_0_fun/ppermute | solution.py:676
  57.3 17.1 %collective-permute-start.12 = (bf16[2,64,2048]{2,1,0:T(8,128)(2,1)}, bf16[2,64,2048]{2,1,0:T(8,128)(2,1)}, u32[]{:S(2)}, u32[]{:S(2)}) collective-permute-start(bf16[2,64,2048]{2,1,0:T(8,128)(2,1)} %get-tuple-element.189), channel_id=1, source_target_pairs={{0,4},{1,5},{2,6},{3,7},{8,12},{9,13},{10,14},{11,15},{4,0},{5,1},... | collective-permute-start | bytes 1572872 | tf_op jit(solution)/shard_map/cond/branch_0_fun/ppermute | solution.py:675
  57.4 19.6 %collective-permute-start.13 = (bf16[2,64,2048]{2,1,0:T(8,128)(2,1)}, bf16[2,64,2048]{2,1,0:T(8,128)(2,1)}, u32[]{:S(2)}, u32[]{:S(2)}) collective-permute-start(bf16[2,64,2048]{2,1,0:T(8,128)(2,1)} %get-tuple-element.190), channel_id=1, source_target_pairs={{4,8},{5,9},{6,10},{7,11},{8,4},{9,5},{10,6},{11,7},{20,24},{21,25... | collective-permute-start | bytes 1572872 | tf_op jit(solution)/shard_map/cond/branch_0_fun/ppermute | solution.py:676
  68.2 14.5 %copy-start.14 = (bf16[128,256]{1,0:T(8,128)(2,1)S(1)}, bf16[128,256]{1,0:T(8,128)(2,1)}, u32[]{:S(2)}) copy-start(bf16[128,256]{1,0:T(8,128)(2,1)} %get-tuple-element.179.image_w_ref) | copy-start | bytes 196612 | tf_op jit(solution)/shard_map/cond
  68.2 14.4 %collective-permute-start.9 = (bf16[1,64,2048]{2,1,0:T(8,128)(2,1)}, bf16[1,64,2048]{2,1,0:T(8,128)(2,1)}, u32[]{:S(2)}, u32[]{:S(2)}) collective-permute-start(bf16[1,64,2048]{2,1,0:T(8,128)(2,1)} %get-tuple-element.183), channel_id=1, source_target_pairs={{0,4},{1,5},{2,6},{3,7},{8,12},{9,13},{10,14},{11,15},{4,0},{5,1},... | collective-permute-start | bytes 786440 | tf_op jit(solution)/shard_map/cond/branch_0_fun/ppermute | solution.py:675
  68.3 14.4 %collective-permute-start.10 = (bf16[1,64,2048]{2,1,0:T(8,128)(2,1)}, bf16[1,64,2048]{2,1,0:T(8,128)(2,1)}, u32[]{:S(2)}, u32[]{:S(2)}) collective-permute-start(bf16[1,64,2048]{2,1,0:T(8,128)(2,1)} %get-tuple-element.184), channel_id=1, source_target_pairs={{4,8},{5,9},{6,10},{7,11},{8,4},{9,5},{10,6},{11,7},{20,24},{21,25... | collective-permute-start | bytes 786440 | tf_op jit(solution)/shard_map/cond/branch_0_fun/ppermute | solution.py:676
  79.4 21.8 %collective-permute-start.14 = (bf16[1,64,2048]{2,1,0:T(8,128)(2,1)}, bf16[1,64,2048]{2,1,0:T(8,128)(2,1)S(1)}, u32[]{:S(2)}, u32[]{:S(2)}) collective-permute-start(bf16[1,64,2048]{2,1,0:T(8,128)(2,1)} %get-tuple-element.191), channel_id=1, source_target_pairs={{0,4},{1,5},{2,6},{3,7},{8,12},{9,13},{10,14},{11,15},{4,0},{5,1},... | collective-permute-start | bytes 786440 | tf_op jit(solution)/shard_map/cond/branch_0_fun/ppermute | solution.py:675
  79.5 21.8 %collective-permute-start.15 = (bf16[1,64,2048]{2,1,0:T(8,128)(2,1)}, bf16[1,64,2048]{2,1,0:T(8,128)(2,1)S(1)}, u32[]{:S(2)}, u32[]{:S(2)}) collective-permute-start(bf16[1,64,2048]{2,1,0:T(8,128)(2,1)} %get-tuple-element.192), channel_id=1, source_target_pairs={{4,8},{5,9},{6,10},{7,11},{8,4},{9,5},{10,6},{11,7},{20,24},{21,25... | collective-permute-start | bytes 786440 | tf_op jit(solution)/shard_map/cond/branch_0_fun/ppermute | solution.py:676
  97.0 20.4 %collective-permute-start.11 = (bf16[16,2048]{1,0:T(8,128)(2,1)}, bf16[16,2048]{1,0:T(8,128)(2,1)S(1)}, u32[]{:S(2)}, u32[]{:S(2)}) collective-permute-start(bf16[16,2048]{1,0:T(8,128)(2,1)} %get-tuple-element.185), channel_id=1, source_target_pairs={{0,1},{1,2},{2,3},{3,4},{4,5},{5,6},{6,7},{7,8},{8,9},{9,10},{10,1... | collective-permute-start | bytes 196616 | tf_op jit(solution)/shard_map/cond/branch_0_fun/ppermute | solution.py:679
  101.3 0.7 copy-start.20
  101.3 0.8 copy-start.22
  117.3 0.6 copy-start.26
